TPU v7x, 32 devices: a whole 2x2x4 slice. The times are simulated.
32 devices in a mesh: dp: 16 (over z, y, x), tensor: 2 (over core).
Axes of the slice: x: 2, y: 2, z: 4, core: 2. Of those that a mesh axis runs over, the one named last changes fastest.
Arguments:
- inputs: bfloat16 [32768, 768], P(('dp', 'tensor')), may hold values from -6 to 6
- out_grad: bfloat16 [32768, 768], P(('dp', 'tensor')), may hold values from -6 to 6
- lengths: int32 [16], P('dp'), may hold values from 1025 to 2048
- w_qkv: bfloat16 [3, 768, 768], P(None, 'dp', 'tensor'), may hold values from -0.21875 to 0.21875
- w_out: bfloat16 [768, 768], P('tensor', 'dp'), may hold values from -1.75 to 1.75
- w_up: bfloat16 [768, 3072], P('dp', 'tensor'), may hold values from -0.21875 to 0.21875
- w_down: bfloat16 [3072, 768], P('tensor', 'dp'), may hold values from -0.109375 to 0.109375
- gains: bfloat16 [2, 768], replicated, may hold values from 0.099609375 to 1.8984375
- shifts: bfloat16 [4, 768], replicated, may hold values from -3 to 3
- ff_bias: bfloat16 [3072], P('tensor'), may hold values from -3 to 3
Outputs:
- out: bfloat16 [32768, 768], P(('dp', 'tensor'))
- grad_inputs: float32 [32768, 768], P(('dp', 'tensor'))
- grad_qkv: float32 [3, 768, 768], P(None, 'dp', 'tensor')
- grad_out_proj: float32 [768, 768], P('tensor', 'dp')
- grad_up: float32 [768, 3072], P('dp', 'tensor')
- grad_down: float32 [3072, 768], P('tensor', 'dp')
- grad_gains: float32 [2, 768], replicated
- grad_shifts: float32 [4, 768], replicated
- grad_ff_bias: float32 [3072], P('tensor')
All inputs are finite; a program needn't handle non-finite values.
Results may differ from a plain program's by a relative error of at most 0.015.
The roundings to bfloat16 on the way count: a program that leaves them out, or rounds other values in their place, can miss the bound.
Values may be sent and summed in bfloat16 or wider, within the bound.
A program may use at most 192 MiB of HBM per device.

v0:
```python
import jax
import jax.numpy as jnp
from jax import lax
from jax.sharding import PartitionSpec as P

HD = 64
LEN = 2048
norm_eps = 1e-06
masked_score = -1e30


def layer_norm(hidden, gain, shift):
    center = hidden - jnp.mean(hidden, axis=-1, keepdims=True)
    spread = jnp.mean(center * center, axis=-1, keepdims=True)
    return center * lax.rsqrt(spread + norm_eps) * gain + shift


def exact_gelu(ff_pre):
    return jax.nn.gelu(ff_pre, approximate=False)


def softmax_rows(query_block, key_rows, key_mask):
    scores = jnp.einsum("qd,kd->qk", query_block, key_rows, preferred_element_type=jnp.float32)
    scores = jnp.where(key_mask[None, :], scores, masked_score)
    row_max = jnp.max(scores, axis=-1, keepdims=True)
    shifted = jnp.exp(scores - row_max)
    return shifted / jnp.sum(shifted, axis=-1, keepdims=True)


def heads_first(matrix, seq_count, head_count):
    return (
        matrix.reshape(seq_count, LEN, head_count, HD)
        .transpose(0, 2, 1, 3)
        .reshape(seq_count * head_count, LEN, HD)
    )


def heads_last(stacked, seq_count, head_count):
    return (
        stacked.reshape(seq_count, head_count, LEN, HD)
        .transpose(0, 2, 1, 3)
        .reshape(seq_count * LEN, head_count * HD)
    )


def attend_forward(member):
    query_rows, key_rows, value_rows, seq_len = member
    key_mask = jnp.arange(LEN, dtype=jnp.int32) < seq_len
    block_rows = min(512, LEN)

    def one_block(query_block):
        attn_probs = softmax_rows(query_block, key_rows, key_mask)
        return jnp.dot(
            attn_probs.astype(jnp.bfloat16), value_rows, preferred_element_type=jnp.float32
        )

    context = lax.map(one_block, query_rows.reshape(LEN // block_rows, block_rows, HD))
    return context.reshape(LEN, HD)


def attend_backward(member):
    query_rows, key_rows, value_rows, ctx_rows, seq_len = member
    key_mask = jnp.arange(LEN, dtype=jnp.int32) < seq_len
    block_rows = min(512, LEN)

    def one_step(totals, blocks):
        key_total, value_total = totals
        query_block, ctx_block = blocks
        attn_probs = softmax_rows(query_block, key_rows, key_mask)
        prob_grad = jnp.einsum(
            "qd,kd->qk", ctx_block, value_rows, preferred_element_type=jnp.float32
        )
        delta = jnp.sum(attn_probs * prob_grad, axis=-1, keepdims=True)
        score_grad = (attn_probs * (prob_grad - delta)).astype(jnp.bfloat16)
        query_part = jnp.einsum(
            "qk,kd->qd", score_grad, key_rows, preferred_element_type=jnp.float32
        )
        key_total = key_total + jnp.einsum(
            "qk,qd->kd", score_grad, query_block, preferred_element_type=jnp.float32
        )
        value_total = value_total + jnp.einsum(
            "qk,qd->kd",
            attn_probs.astype(jnp.bfloat16),
            ctx_block,
            preferred_element_type=jnp.float32,
        )
        return ((key_total, value_total), query_part)

    zeros_init = jnp.zeros((LEN, HD), jnp.float32)
    shaped = (LEN // block_rows, block_rows, HD)
    (key_grad, value_grad), query_grad = lax.scan(
        one_step, (zeros_init, zeros_init), (query_rows.reshape(shaped), ctx_rows.reshape(shaped))
    )
    return (query_grad.reshape(LEN, HD), key_grad, value_grad)


def body(inputs, out_grad, lengths, w_qkv, w_out, w_up, w_down, gains, shifts, ff_bias):
    score_scale = HD ** (-0.5)
    seq_count = lengths.shape[0]
    head_count = w_qkv.shape[2] // HD
    gains_f = gains.astype(jnp.float32)
    shifts_f = shifts.astype(jnp.float32)
    inputs_f = inputs.astype(jnp.float32)
    gathered = lax.all_gather(inputs, "tensor", axis=0, tiled=True)
    qkv_full, out_full = (
        lax.all_gather(w_qkv, "dp", axis=1, tiled=True),
        lax.all_gather(w_out, "dp", axis=1, tiled=True),
    )
    projected = jnp.einsum("rd,cde->cre", gathered, qkv_full, preferred_element_type=jnp.float32)
    queries = (projected[0] * score_scale).astype(jnp.bfloat16)
    keys_all = projected[1].astype(jnp.bfloat16)
    values_all = projected[2].astype(jnp.bfloat16)
    head_lens = jnp.repeat(lengths, head_count)
    query_heads = heads_first(queries, seq_count, head_count)
    key_heads = heads_first(keys_all, seq_count, head_count)
    value_heads = heads_first(values_all, seq_count, head_count)
    context_f = lax.map(attend_forward, (query_heads, key_heads, value_heads, head_lens))
    context = heads_last(context_f, seq_count, head_count).astype(jnp.bfloat16)
    attn_branch = (
        lax.psum_scatter(
            jnp.dot(context, out_full, preferred_element_type=jnp.float32),
            "tensor",
            scatter_dimension=0,
            tiled=True,
        )
        + shifts_f[0]
    )
    resid_one = inputs_f + attn_branch
    normed_f, norm_one_back = jax.vjp(layer_norm, resid_one, gains_f[0], shifts_f[1])
    normed_one = normed_f.astype(jnp.bfloat16)
    normed_all = lax.all_gather(normed_one, "tensor", axis=0, tiled=True)
    up_full, down_full = (
        lax.all_gather(w_up, "dp", axis=0, tiled=True),
        lax.all_gather(w_down, "dp", axis=1, tiled=True),
    )
    ff_pre = jnp.dot(normed_all, up_full, preferred_element_type=jnp.float32) + ff_bias.astype(
        jnp.float32
    )
    ff_act_f, gelu_back = jax.vjp(exact_gelu, ff_pre)
    ff_act = ff_act_f.astype(jnp.bfloat16)
    mlp_branch = (
        lax.psum_scatter(
            jnp.dot(ff_act, down_full, preferred_element_type=jnp.float32),
            "tensor",
            scatter_dimension=0,
            tiled=True,
        )
        + shifts_f[2]
    )
    resid_two = normed_one.astype(jnp.float32) + mlp_branch
    result, norm_two_back = jax.vjp(layer_norm, resid_two, gains_f[1], shifts_f[3])
    resid_two_grad, gain_two_grad, shift_three_grad = norm_two_back(out_grad.astype(jnp.float32))
    mlp_grad = resid_two_grad.astype(jnp.bfloat16)
    shift_two_grad = jnp.sum(mlp_grad.astype(jnp.float32), axis=0)
    mlp_grad_all = lax.all_gather(mlp_grad, "tensor", axis=0, tiled=True)
    act_grad = jnp.einsum("rd,fd->rf", mlp_grad_all, down_full, preferred_element_type=jnp.float32)
    down_grad = jnp.einsum("rf,rd->fd", ff_act, mlp_grad_all, preferred_element_type=jnp.float32)
    pre_grad = gelu_back(act_grad)[0].astype(jnp.bfloat16)
    bias_grad = jnp.sum(pre_grad.astype(jnp.float32), axis=0)
    up_grad = jnp.einsum("rd,rf->df", normed_all, pre_grad, preferred_element_type=jnp.float32)
    slab_rows = pre_grad
    normed_grad = resid_two_grad + lax.psum_scatter(
        jnp.einsum("rf,df->rd", slab_rows, up_full, preferred_element_type=jnp.float32),
        "tensor",
        scatter_dimension=0,
        tiled=True,
    )
    resid_one_grad, gain_one_grad, shift_one_grad = norm_one_back(normed_grad)
    attn_grad = resid_one_grad.astype(jnp.bfloat16)
    shift_zero_grad = jnp.sum(attn_grad.astype(jnp.float32), axis=0)
    attn_grad_all = lax.all_gather(attn_grad, "tensor", axis=0, tiled=True)
    context_grad = jnp.einsum(
        "rd,ed->re", attn_grad_all, out_full, preferred_element_type=jnp.float32
    ).astype(jnp.bfloat16)
    out_proj_grad = jnp.einsum(
        "re,rd->ed", context, attn_grad_all, preferred_element_type=jnp.float32
    )
    ctx_heads = heads_first(context_grad, seq_count, head_count)
    query_grad, key_grad, value_grad = lax.map(
        attend_backward, (query_heads, key_heads, value_heads, ctx_heads, head_lens)
    )
    stacked_grad = jnp.stack(
        [
            heads_last(query_grad, seq_count, head_count),
            heads_last(key_grad, seq_count, head_count),
            heads_last(value_grad, seq_count, head_count),
        ]
    ).astype(jnp.bfloat16)
    qkv_scale = jnp.array([score_scale, 1.0, 1.0], jnp.float32)
    qkv_grad = (
        jnp.einsum("rd,cre->cde", gathered, stacked_grad, preferred_element_type=jnp.float32)
        * qkv_scale[:, None, None]
    )
    qkv_owned, out_owned, up_owned, down_owned = (
        lax.psum_scatter(qkv_grad, "dp", scatter_dimension=1, tiled=True),
        lax.psum_scatter(out_proj_grad, "dp", scatter_dimension=1, tiled=True),
        lax.psum_scatter(up_grad, "dp", scatter_dimension=0, tiled=True),
        lax.psum_scatter(down_grad, "dp", scatter_dimension=1, tiled=True),
    )
    slab_rows = stacked_grad
    parts = jnp.einsum("cre,cde->crd", slab_rows, qkv_full, preferred_element_type=jnp.float32)
    input_grad = resid_one_grad + lax.psum_scatter(
        (parts[0] * score_scale + parts[1] + parts[2]).astype(jnp.bfloat16),
        "tensor",
        scatter_dimension=0,
        tiled=True,
    ).astype(jnp.float32)
    gain_grads = jnp.stack([gain_one_grad, gain_two_grad])
    shift_grads = jnp.stack([shift_zero_grad, shift_one_grad, shift_two_grad, shift_three_grad])
    tensor_count = lax.axis_size("tensor")
    own_slot = (jnp.arange(tensor_count, dtype=jnp.int32) == lax.axis_index("tensor")).astype(
        jnp.float32
    )
    spread_bias = own_slot[:, None] * bias_grad[None, :]
    gain_sum, shift_sum, bias_sum = lax.psum(
        (gain_grads, shift_grads, spread_bias), ("dp", "tensor")
    )
    bias_owned = jnp.sum(own_slot[:, None] * bias_sum, axis=0)
    return (
        result.astype(jnp.bfloat16),
        input_grad,
        qkv_owned,
        out_owned,
        up_owned,
        down_owned,
        gain_sum,
        shift_sum,
        bias_owned,
    )


def solution(mesh):
    return jax.shard_map(
        body,
        mesh=mesh,
        in_specs=(
            P(("dp", "tensor"), None),
            P(("dp", "tensor"), None),
            P("dp"),
            P(None, "dp", "tensor"),
            P("tensor", "dp"),
            P("dp", "tensor"),
            P("tensor", "dp"),
            P(),
            P(),
            P("tensor"),
        ),
        out_specs=(
            P(("dp", "tensor"), None),
            P(("dp", "tensor"), None),
            P(None, "dp", "tensor"),
            P("tensor", "dp"),
            P("dp", "tensor"),
            P("tensor", "dp"),
            P(),
            P(),
            P("tensor"),
        ),
        check_vma=False,
    )
```

profile of v0, /device:TPU:0, one launch (start us, length us, event | category | flops | bytes accessed | tf_op | source)
XLA Modules:
  0.0 1468.2 jit_solution(2063813809935758152)
XLA Ops:
  9.4 48.6 %all_gather.26 = bf16[384,768]{0,1:T(8,128)(2,1)} all-gather(bf16[384,48]{0,1:T(8,128)(2,1)} %param.23), channel_id=1, replica_groups=mesh['dp'=16,'tensor'=2] {'dp'}, dimensions={1}, use_global_device_ids=true | all-gather | bytes 626688 | tf_op jit(solution)/shard_map/all_gather | solution.py:107
  58.0 29.4 %all-gather.8.cloned.1.call-done = bf16[3,768,384]{2,1,0:T(8,128)(2,1)} async-done(((bf16[3,48,384]{2,1,0:T(8,128)(2,1)}), bf16[3,768,384]{2,1,0:T(8,128)(2,1)}) %all-gather.8.cloned.1.call-update) | async-done | bytes 1769488 | tf_op jit(solution)/shard_map/all_gather | solution.py:106
  108.1 103.9 %while.51 = (s32[]{:T(128)}, bf16[6,2048,64]{1,2,0:T(8,128)(2,1)S(1)}, bf16[6,2048,64]{2,1,0:T(8,128)(2,1)}, bf16[6,2048,64]{2,1,0:T(8,128)(2,1)}, s32[6]{0:T(12...) while((s32[]{:T(128)}, bf16[6,2048,64]{1,2,0:T(8,128)(2,1)S(1)}, ...), condition=%wide.region_5.6_spmd, body=%wide.region_0.5_spmd.sunk | while | flops 277873664 | bytes 17058060 | solution.py:117
  128.4 13.8 while.54
  145.7 13.8 while.54
  163.1 13.8 while.54
  180.4 13.8 while.54
  237.9 60.2 %all-gather.14.cloned.1.call-done = bf16[768,1536]{1,0:T(8,128)(2,1)} async-done(((bf16[48,1536]{1,0:T(8,128)(2,1)}), bf16[768,1536]{1,0:T(8,128)(2,1)}) %all-gather.14.cloned.1.call-update) | async-done | bytes 2359312 | tf_op jit(solution)/shard_map/all_gather | solution.py:133
  311.1 34.9 %multiply_convert_fusion.1 = (bf16[2048,1536]{1,0:T(8,128)(2,1)}, f32[2048,1536]{1,0:T(8,128)}, f32[2048,1536]{1,0:T(8,128)}) fusion(f32[1536]{0:T(1024)S(1)} %convert_element_type.134, bf16[2048,768]{1,0:T(8,128)(2,1)} %all-gather.12.cloned.1.call-done, bf16[768,1536]{1,0:T(8,128)(2,1)} %all-gather.14.cloned.1.call-done), kind=kOutput, calls=%fused_computation.56 | convolution fusion | flops 5039456256 | bytes 36968448 | tf_op jit(solution)/shard_map/dot_general | solution.py:136
  346.0 31.7 %all-gather.16.cloned.1.call-done = bf16[1536,768]{0,1:T(8,128)(2,1)} async-done(((bf16[1536,48]{0,1:T(8,128)(2,1)}), bf16[1536,768]{0,1:T(8,128)(2,1)}) %all-gather.16.cloned.1.call-update) | async-done | bytes 2359312 | tf_op jit(solution)/shard_map/all_gather | solution.py:134
  426.6 17.6 %convert_reduce_fusion = (f32[1536]{0:T(1024)}, bf16[2048,1536]{1,0:T(8,128)(2,1)S(1)}) fusion(f32[2048,1536]{1,0:T(8,128)} %get-tuple-element.382, bf16[2048,768]{1,0:T(8,128)(2,1)} %all-gather.18.cloned.1.call-done, bf16[1536,768]{0,1:T(8,128)(2,1)} %all-gather.16.cloned.1.call-done, f32[2048,1536]{1,0:T(8,128)} %get-tuple-element.400, ...), kind=kOutput, calls=%fused_computation.54 | convolution fusion | flops 4885314048 | bytes 36974592 | tf_op jit(solution)/shard_map/rd,fd->rf/dot_general | solution.py:156
  453.9 15.8 %reduce-scatter.12.cloned.1.call-done = f32[1024,768]{1,0:T(8,128)} async-done(((f32[2048,768]{1,0:T(8,128)}), f32[1024,768]{1,0:T(8,128)}) %reduce-scatter.12.cloned.1.call-update) | async-done | bytes 3145744 | tf_op jit(solution)/shard_map/reduce_scatter | solution.py:162
  503.3 328.2 %while.53 = (s32[]{:T(128)}, bf16[6,2048,64]{1,2,0:T(8,128)(2,1)}, bf16[6,2048,64]{1,2,0:T(8,128)(2,1)}, bf16[6,2048,64]{1,2,0:T(8,128)(2,1)}, bf16[6,2048,64]{2...) while((s32[]{:T(128)}, bf16[6,2048,64]{1,2,0:T(8,128)(2,1)}, ...), condition=%wide.region_23.24_spmd, body=%wide.region_17.23_spmd.sunk | while | flops 692584960 | bytes 79334840 | solution.py:179
  508.2 47.7 %while.55 = (s32[]{:T(128)}, f32[2048,64]{0,1:T(8,128)S(1)}, f32[2048,64]{0,1:T(8,128)S(1)}, bf16[4,512,64]{1,2,0:T(8,128)(2,1)S(1)}, bf16[4,512,64]{2,1,0:T(8,1...) while((s32[]{:T(128)}, f32[2048,64]{0,1:T(8,128)S(1)}, ...), condition=%wide.region_22.22_spmd.clone, body=%wide.region_18.21_spmd.clone.sunk | while | flops 692584960 | bytes 73566400 | solution.py:91
  562.9 47.7 %while.55 = (s32[]{:T(128)}, f32[2048,64]{0,1:T(8,128)S(1)}, f32[2048,64]{0,1:T(8,128)S(1)}, bf16[4,512,64]{1,2,0:T(8,128)(2,1)S(1)}, bf16[4,512,64]{2,1,0:T(8,1...) while((s32[]{:T(128)}, f32[2048,64]{0,1:T(8,128)S(1)}, ...), condition=%wide.region_22.22_spmd.clone, body=%wide.region_18.21_spmd.clone.sunk | while | flops 692584960 | bytes 73566400 | solution.py:91
  617.6 47.7 %while.55 = (s32[]{:T(128)}, f32[2048,64]{0,1:T(8,128)S(1)}, f32[2048,64]{0,1:T(8,128)S(1)}, bf16[4,512,64]{1,2,0:T(8,128)(2,1)S(1)}, bf16[4,512,64]{2,1,0:T(8,1...) while((s32[]{:T(128)}, f32[2048,64]{0,1:T(8,128)S(1)}, ...), condition=%wide.region_22.22_spmd.clone, body=%wide.region_18.21_spmd.clone.sunk | while | flops 692584960 | bytes 73566400 | solution.py:91
  672.4 47.7 %while.55 = (s32[]{:T(128)}, f32[2048,64]{0,1:T(8,128)S(1)}, f32[2048,64]{0,1:T(8,128)S(1)}, bf16[4,512,64]{1,2,0:T(8,128)(2,1)S(1)}, bf16[4,512,64]{2,1,0:T(8,1...) while((s32[]{:T(128)}, f32[2048,64]{0,1:T(8,128)S(1)}, ...), condition=%wide.region_22.22_spmd.clone, body=%wide.region_18.21_spmd.clone.sunk | while | flops 692584960 | bytes 73566400 | solution.py:91
  727.0 47.7 %while.55 = (s32[]{:T(128)}, f32[2048,64]{0,1:T(8,128)S(1)}, f32[2048,64]{0,1:T(8,128)S(1)}, bf16[4,512,64]{1,2,0:T(8,128)(2,1)S(1)}, bf16[4,512,64]{2,1,0:T(8,1...) while((s32[]{:T(128)}, f32[2048,64]{0,1:T(8,128)S(1)}, ...), condition=%wide.region_22.22_spmd.clone, body=%wide.region_18.21_spmd.clone.sunk | while | flops 692584960 | bytes 73566400 | solution.py:91
  781.7 47.7 %while.55 = (s32[]{:T(128)}, f32[2048,64]{0,1:T(8,128)S(1)}, f32[2048,64]{0,1:T(8,128)S(1)}, bf16[4,512,64]{1,2,0:T(8,128)(2,1)S(1)}, bf16[4,512,64]{2,1,0:T(8,1...) while((s32[]{:T(128)}, f32[2048,64]{0,1:T(8,128)S(1)}, ...), condition=%wide.region_22.22_spmd.clone, body=%wide.region_18.21_spmd.clone.sunk | while | flops 692584960 | bytes 73566400 | solution.py:91
  892.1 42.1 %all-reduce.1 = (f32[2,768]{1,0:T(2,128)}, f32[4,768]{1,0:T(4,128)}, f32[2,1536]{1,0:T(2,128)S(1)}) all-reduce(f32[2,768]{1,0:T(2,128)S(1)} %pad_maximum_fusion.4, f32[4,768]{1,0:T(4,128)S(1)} %pad_maximum_fusion.3, f32[2,1536]{1,0:T(2,128)S(1)} %broadcast_multiply_fusion), channel_id=1, replica_groups=mesh['dp'=16,'tensor'=2] {'dp','tensor'}, use_global_device_ids=true, to_apply=%region_31.32 | all-reduce | flops 7680 | bytes 61440 | tf_op jit(solution)/shard_map/psum | solution.py:215
  934.9 98.8 %all-reduce.4.cloned.1.call-done = f32[3,768,384]{2,0,1:T(4,128)} async-done(((f32[3,768,384]{2,0,1:T(4,128)}), f32[3,768,384]{2,0,1:T(4,128)}) %all-reduce.4.cloned.1.call-update) | async-done | bytes 3538960
  1049.8 141.5 %reduce-scatter.20.cloned.1.call-done = f32[1536,48]{0,1:T(8,128)} async-done(((f32[1536,768]{0,1:T(8,128)}), f32[1536,48]{0,1:T(8,128)}) %reduce-scatter.20.cloned.1.call-update) | async-done | bytes 294928 | tf_op jit(solution)/shard_map/reduce_scatter | solution.py:198
  1191.3 141.8 %reduce-scatter.18.cloned.1.call-done = f32[48,1536]{1,0:T(8,128)} async-done(((f32[768,1536]{1,0:T(8,128)}), f32[48,1536]{1,0:T(8,128)}) %reduce-scatter.18.cloned.1.call-update) | async-done | bytes 294928 | tf_op jit(solution)/shard_map/reduce_scatter | solution.py:197
  1333.0 128.4 %reduce-scatter.16.cloned.1.call-done = f32[384,48]{0,1:T(8,128)} async-done(((f32[384,768]{0,1:T(8,128)}), f32[384,48]{0,1:T(8,128)}) %reduce-scatter.16.cloned.1.call-update) | async-done | bytes 73744 | tf_op jit(solution)/shard_map/reduce_scatter | solution.py:196
  (658 shorter events, 686.6 us)
Async XLA Ops:
  7.2 50.8 %all-gather.10.cloned.1.call-start = ((), (), s32[]{:S(2)}) async-start(), calls=%async_computation.8 | async-start | bytes 4718592 | tf_op jit(solution)/shard_map/all_gather | solution.py:104
  7.9 79.5 %all-gather.8.cloned.1.call-start = ((), (), s32[]{:S(2)}) async-start(), calls=%async_computation.7 | async-start | bytes 1880064 | tf_op jit(solution)/shard_map/all_gather | solution.py:106
  8.7 222.9 %reduce-scatter.8.cloned.1.call-start = ((), (), s32[]{:S(2)}) async-start(), calls=%async_computation.9 | async-start | bytes 9437184 | tf_op jit(solution)/shard_map/reduce_scatter | solution.py:120
  218.1 80.0 %all-gather.14.cloned.1.call-start = ((), (), s32[]{:S(2)}) async-start(), calls=%async_computation.11 | async-start | bytes 2506752 | tf_op jit(solution)/shard_map/all_gather | solution.py:133
  218.7 92.4 %all-gather.12.cloned.1.call-start = ((), (), s32[]{:S(2)}) async-start(), calls=%async_computation.10 | async-start | bytes 4718592 | tf_op jit(solution)/shard_map/all_gather | solution.py:131
  237.2 140.4 %all-gather.16.cloned.1.call-start = ((), (), s32[]{:S(2)}) async-start(), calls=%async_computation.12 | async-start | bytes 2506752 | tf_op jit(solution)/shard_map/all_gather | solution.py:134
  237.8 163.0 %reduce-scatter.10.cloned.1.call-start = ((), (), s32[]{:S(2)}) async-start(), calls=%async_computation.13 | async-start | bytes 9437184 | tf_op jit(solution)/shard_map/reduce_scatter | solution.py:142
  387.3 39.3 %all-gather.18.cloned.1.call-start = ((), (), s32[]{:S(2)}) async-start(), calls=%async_computation.14 | async-start | bytes 4718592 | tf_op jit(solution)/shard_map/all_gather | solution.py:155
  413.2 56.4 %reduce-scatter.12.cloned.1.call-start = ((), (), s32[]{:S(2)}) async-start(), calls=%async_computation.15 | async-start | bytes 9437184 | tf_op jit(solution)/shard_map/reduce_scatter | solution.py:162
  426.6 20.2 %copy-start.24 = (bf16[768,1536]{1,0:T(8,128)(2,1)S(1)}, bf16[768,1536]{1,0:T(8,128)(2,1)}, u32[]{:S(2)}) copy-start(bf16[768,1536]{1,0:T(8,128)(2,1)} %all-gather.14.cloned.1.call-done) | copy-start | bytes 7077892
  453.8 20.1 %copy-start.11 = (f32[1024]{0:T(1024)S(1)}, f32[1024]{0:T(1024)}, u32[]{:S(2)}) copy-start(f32[1024]{0:T(1024)} %copy-done.10) | copy-start | bytes 12292
  453.8 38.8 %all-gather.20.cloned.1.call-start = ((), (), s32[]{:S(2)}) async-start(), calls=%async_computation.16 | async-start | bytes 4718592 | tf_op jit(solution)/shard_map/all_gather | solution.py:171
  477.0 15.6 %copy-start.7 = (bf16[384,768]{0,1:T(8,128)(2,1)S(1)}, bf16[384,768]{0,1:T(8,128)(2,1)}, u32[]{:S(2)}) copy-start(bf16[384,768]{0,1:T(8,128)(2,1)} %all_gather.26) | copy-start | bytes 1769476
  479.2 554.5 %all-reduce.4.cloned.1.call-start = ((), (), s32[]{:S(2)}) async-start(), calls=%async_computation.21 | async-start | bytes 9437184
  852.4 194.0 %reduce-scatter.14.cloned.1.call-start = ((), (), s32[]{:S(2)}) async-start(), calls=%async_computation.17 | async-start | bytes 4718592 | tf_op jit(solution)/shard_map/reduce_scatter | solution.py:202
  862.1 329.1 %reduce-scatter.20.cloned.1.call-start = ((), (), s32[]{:S(2)}) async-start(), calls=%async_computation.20 | async-start | bytes 5013504 | tf_op jit(solution)/shard_map/reduce_scatter | solution.py:198
  873.5 459.5 %reduce-scatter.18.cloned.1.call-start = ((), (), s32[]{:S(2)}) async-start(), calls=%async_computation.19 | async-start | bytes 5013504 | tf_op jit(solution)/shard_map/reduce_scatter | solution.py:197
  885.1 6.9 copy-start.18
  885.1 7.0 copy-start.17
  885.1 7.0 copy-start.13
  885.1 7.0 copy-start.12
  885.1 161.3 %copy-start.9 = (f32[1024]{0:T(1024)S(1)}, f32[1024]{0:T(1024)}, u32[]{:S(2)}) copy-start(f32[1024]{0:T(1024)} %copy-done.8) | copy-start | bytes 12292
  885.1 576.3 %reduce-scatter.16.cloned.1.call-start = ((), (), s32[]{:S(2)}) async-start(), calls=%async_computation.18 | async-start | bytes 1253376 | tf_op jit(solution)/shard_map/reduce_scatter | solution.py:196
  885.2 161.2 %copy-start.3 = (f32[1024,768]{1,0:T(8,128)S(1)}, f32[1024,768]{1,0:T(8,128)}, u32[]{:S(2)}) copy-start(f32[1024,768]{1,0:T(8,128)} %copy-done.2) | copy-start | bytes 9437188
  (67 other events, 198.9 us)
Sparse Core Ops, SparseCore 0:
  9.6 14.8 all-gather.9
  27.1 60.2 all-gather.7
  218.3 13.2 reduce-scatter.7
  234.6 63.4 all-gather.13
  300.1 10.9 all-gather.11
  314.1 63.4 all-gather.15
  387.4 13.3 reduce-scatter.9
  413.3 13.2 all-gather.17
  453.9 15.6 reduce-scatter.11
  479.3 13.2 all-gather.19
  852.5 181.1 all-reduce.3
  1036.4 9.9 reduce-scatter.13
  1052.9 138.3 reduce-scatter.19
  1196.9 136.1 reduce-scatter.17
  1338.9 122.4 reduce-scatter.15
where the time goes:
time: 1480 us; the launch traced here: 1470 us
  waiting for transfers between devices  727 us (49%)
  matrix products  341 us (23%)
  local copies, waits for them, and re-layouts  154 us (10%)
  other arithmetic  136 us (9%)
  blocking collectives  90.7 us (6%)
  between operations  15.8 us (1%)
    reduce_scatter x1, waiting for transfers between devices, body(): lax.psum_scatter(up_grad, 'dp', scatter_dimension=0, tiled=True)  142 us
    reduce_scatter x1, waiting for transfers between devices, body(): lax.psum_scatter(down_grad, 'dp', scatter_dimension=1, tiled=True)  141 us
    reduce_scatter x1, waiting for transfers between devices, body(): lax.psum_scatter(out_proj_grad, 'dp', scatter_dimension=1, tiled=True)  128 us
    unnamed x16, waiting for transfers between devices  101 us
    dot_general x24, matrix products, one_step(): jnp.einsum('qk,qd->kd', attn_probs.astype(jnp.bfloat16), ctx_block, prefe...  83 us
    all_gather x1, waiting for transfers between devices, body(): lax.all_gather(w_up, 'dp', axis=0, tiled=True)  60.2 us
    while x96, local copies, waits for them, and re-layouts  49 us
    all_gather x1, blocking collectives, body(): lax.all_gather(w_out, 'dp', axis=1, tiled=True)  48.6 us
  transfers between devices with their start and end apart: 15, of which 14 were waited for; matrix products, arithmetic and copies ran while one was open for 5% of the time, Pallas kernels for 0%

commit v1 on v0

--- a/solution.py
+++ b/solution.py
@@ -213,7 +213,7 @@
     )
     spread_bias = own_slot[:, None] * bias_grad[None, :]
     gain_sum, shift_sum, bias_sum = lax.psum(
-        (gain_grads, shift_grads, spread_bias), ("dp", "tensor")
+        lax.psum((gain_grads, shift_grads, spread_bias), "dp"), "tensor"
     )
     bias_owned = jnp.sum(own_slot[:, None] * bias_sum, axis=0)
     return (

time: 1480 us -> 1480 us (level)
  waiting for transfers between devices: 727 us -> 687 us
  blocking collectives: 90.7 us -> 130 us
    unnamed x16, waiting for transfers between devices: 101 us -> 62 us
    psum x1 -> x2, blocking collectives: 42.1 us -> 81.4 us  [the longest x1 77.4 us: body(): lax.psum((gain_grads, shift_grads, spread_bias), 'dp')]
where the time goes in v1:
time: 1480 us; the launch traced here: 1470 us
  waiting for transfers between devices  687 us (46%)
  matrix products  341 us (23%)
  local copies, waits for them, and re-layouts  154 us (10%)
  other arithmetic  136 us (9%)
  blocking collectives  130 us (9%)
  between operations  15.8 us (1%)
    reduce_scatter x1, waiting for transfers between devices, body(): lax.psum_scatter(up_grad, 'dp', scatter_dimension=0, tiled=True)  142 us
    reduce_scatter x1, waiting for transfers between devices, body(): lax.psum_scatter(down_grad, 'dp', scatter_dimension=1, tiled=True)  142 us
    reduce_scatter x1, waiting for transfers between devices, body(): lax.psum_scatter(out_proj_grad, 'dp', scatter_dimension=1, tiled=True)  129 us
    dot_general x24, matrix products, one_step(): jnp.einsum('qk,qd->kd', attn_probs.astype(jnp.bfloat16), ctx_block, prefe...  83 us
    psum x1, blocking collectives, body(): lax.psum((gain_grads, shift_grads, spread_bias), 'dp')  77.4 us
    unnamed x16, waiting for transfers between devices  62 us
    all_gather x1, waiting for transfers between devices, body(): lax.all_gather(w_up, 'dp', axis=0, tiled=True)  60.2 us
    while x96, local copies, waits for them, and re-layouts  49 us
  transfers between devices with their start and end apart: 15, of which 14 were waited for; matrix products, arithmetic and copies ran while one was open for 5% of the time, Pallas kernels for 0%

profile of v1, /device:TPU:0, one launch (start us, length us, event | category | flops | bytes accessed | tf_op | source)
XLA Modules:
  0.0 1468.2 jit_solution(6563611922266266938)
XLA Ops:
  9.4 48.6 %all_gather.26 = bf16[384,768]{0,1:T(8,128)(2,1)} all-gather(bf16[384,48]{0,1:T(8,128)(2,1)} %param.23), channel_id=1, replica_groups=mesh['dp'=16,'tensor'=2] {'dp'}, dimensions={1}, use_global_device_ids=true | all-gather | bytes 626688 | tf_op jit(solution)/shard_map/all_gather | solution.py:107
  58.0 29.4 %all-gather.8.cloned.1.call-done = bf16[3,768,384]{2,1,0:T(8,128)(2,1)} async-done(((bf16[3,48,384]{2,1,0:T(8,128)(2,1)}), bf16[3,768,384]{2,1,0:T(8,128)(2,1)}) %all-gather.8.cloned.1.call-update) | async-done | bytes 1769488 | tf_op jit(solution)/shard_map/all_gather | solution.py:106
  108.1 103.9 %while.51 = (s32[]{:T(128)}, bf16[6,2048,64]{1,2,0:T(8,128)(2,1)S(1)}, bf16[6,2048,64]{2,1,0:T(8,128)(2,1)}, bf16[6,2048,64]{2,1,0:T(8,128)(2,1)}, s32[6]{0:T(12...) while((s32[]{:T(128)}, bf16[6,2048,64]{1,2,0:T(8,128)(2,1)S(1)}, ...), condition=%wide.region_5.6_spmd, body=%wide.region_0.5_spmd.sunk | while | flops 277873664 | bytes 17058060 | solution.py:117
  128.4 13.8 while.54
  145.7 13.8 while.54
  163.1 13.8 while.54
  180.4 13.8 while.54
  237.9 60.2 %all-gather.14.cloned.1.call-done = bf16[768,1536]{1,0:T(8,128)(2,1)} async-done(((bf16[48,1536]{1,0:T(8,128)(2,1)}), bf16[768,1536]{1,0:T(8,128)(2,1)}) %all-gather.14.cloned.1.call-update) | async-done | bytes 2359312 | tf_op jit(solution)/shard_map/all_gather | solution.py:133
  311.1 34.9 %multiply_convert_fusion.1 = (bf16[2048,1536]{1,0:T(8,128)(2,1)}, f32[2048,1536]{1,0:T(8,128)}, f32[2048,1536]{1,0:T(8,128)}) fusion(f32[1536]{0:T(1024)S(1)} %convert_element_type.134, bf16[2048,768]{1,0:T(8,128)(2,1)} %all-gather.12.cloned.1.call-done, bf16[768,1536]{1,0:T(8,128)(2,1)} %all-gather.14.cloned.1.call-done), kind=kOutput, calls=%fused_computation.56 | convolution fusion | flops 5039456256 | bytes 36968448 | tf_op jit(solution)/shard_map/dot_general | solution.py:136
  346.0 31.7 %all-gather.16.cloned.1.call-done = bf16[1536,768]{0,1:T(8,128)(2,1)} async-done(((bf16[1536,48]{0,1:T(8,128)(2,1)}), bf16[1536,768]{0,1:T(8,128)(2,1)}) %all-gather.16.cloned.1.call-update) | async-done | bytes 2359312 | tf_op jit(solution)/shard_map/all_gather | solution.py:134
  426.6 17.6 %convert_reduce_fusion = (f32[1536]{0:T(1024)}, bf16[2048,1536]{1,0:T(8,128)(2,1)S(1)}) fusion(f32[2048,1536]{1,0:T(8,128)} %get-tuple-element.385, bf16[2048,768]{1,0:T(8,128)(2,1)} %all-gather.18.cloned.1.call-done, bf16[1536,768]{0,1:T(8,128)(2,1)} %all-gather.16.cloned.1.call-done, f32[2048,1536]{1,0:T(8,128)} %get-tuple-element.403, ...), kind=kOutput, calls=%fused_computation.54 | convolution fusion | flops 4885314048 | bytes 36974592 | tf_op jit(solution)/shard_map/rd,fd->rf/dot_general | solution.py:156
  453.9 15.8 %reduce-scatter.12.cloned.1.call-done = f32[1024,768]{1,0:T(8,128)} async-done(((f32[2048,768]{1,0:T(8,128)}), f32[1024,768]{1,0:T(8,128)}) %reduce-scatter.12.cloned.1.call-update) | async-done | bytes 3145744 | tf_op jit(solution)/shard_map/reduce_scatter | solution.py:162
  503.3 328.2 %while.53 = (s32[]{:T(128)}, bf16[6,2048,64]{1,2,0:T(8,128)(2,1)}, bf16[6,2048,64]{1,2,0:T(8,128)(2,1)}, bf16[6,2048,64]{1,2,0:T(8,128)(2,1)}, bf16[6,2048,64]{2...) while((s32[]{:T(128)}, bf16[6,2048,64]{1,2,0:T(8,128)(2,1)}, ...), condition=%wide.region_23.24_spmd, body=%wide.region_17.23_spmd.sunk | while | flops 692584960 | bytes 79334840 | solution.py:179
  508.2 47.7 %while.55 = (s32[]{:T(128)}, f32[2048,64]{0,1:T(8,128)S(1)}, f32[2048,64]{0,1:T(8,128)S(1)}, bf16[4,512,64]{1,2,0:T(8,128)(2,1)S(1)}, bf16[4,512,64]{2,1,0:T(8,1...) while((s32[]{:T(128)}, f32[2048,64]{0,1:T(8,128)S(1)}, ...), condition=%wide.region_22.22_spmd.clone, body=%wide.region_18.21_spmd.clone.sunk | while | flops 692584960 | bytes 73566400 | solution.py:91
  562.9 47.7 %while.55 = (s32[]{:T(128)}, f32[2048,64]{0,1:T(8,128)S(1)}, f32[2048,64]{0,1:T(8,128)S(1)}, bf16[4,512,64]{1,2,0:T(8,128)(2,1)S(1)}, bf16[4,512,64]{2,1,0:T(8,1...) while((s32[]{:T(128)}, f32[2048,64]{0,1:T(8,128)S(1)}, ...), condition=%wide.region_22.22_spmd.clone, body=%wide.region_18.21_spmd.clone.sunk | while | flops 692584960 | bytes 73566400 | solution.py:91
  617.6 47.7 %while.55 = (s32[]{:T(128)}, f32[2048,64]{0,1:T(8,128)S(1)}, f32[2048,64]{0,1:T(8,128)S(1)}, bf16[4,512,64]{1,2,0:T(8,128)(2,1)S(1)}, bf16[4,512,64]{2,1,0:T(8,1...) while((s32[]{:T(128)}, f32[2048,64]{0,1:T(8,128)S(1)}, ...), condition=%wide.region_22.22_spmd.clone, body=%wide.region_18.21_spmd.clone.sunk | while | flops 692584960 | bytes 73566400 | solution.py:91
  672.4 47.7 %while.55 = (s32[]{:T(128)}, f32[2048,64]{0,1:T(8,128)S(1)}, f32[2048,64]{0,1:T(8,128)S(1)}, bf16[4,512,64]{1,2,0:T(8,128)(2,1)S(1)}, bf16[4,512,64]{2,1,0:T(8,1...) while((s32[]{:T(128)}, f32[2048,64]{0,1:T(8,128)S(1)}, ...), condition=%wide.region_22.22_spmd.clone, body=%wide.region_18.21_spmd.clone.sunk | while | flops 692584960 | bytes 73566400 | solution.py:91
  727.0 47.7 %while.55 = (s32[]{:T(128)}, f32[2048,64]{0,1:T(8,128)S(1)}, f32[2048,64]{0,1:T(8,128)S(1)}, bf16[4,512,64]{1,2,0:T(8,128)(2,1)S(1)}, bf16[4,512,64]{2,1,0:T(8,1...) while((s32[]{:T(128)}, f32[2048,64]{0,1:T(8,128)S(1)}, ...), condition=%wide.region_22.22_spmd.clone, body=%wide.region_18.21_spmd.clone.sunk | while | flops 692584960 | bytes 73566400 | solution.py:91
  781.7 47.7 %while.55 = (s32[]{:T(128)}, f32[2048,64]{0,1:T(8,128)S(1)}, f32[2048,64]{0,1:T(8,128)S(1)}, bf16[4,512,64]{1,2,0:T(8,128)(2,1)S(1)}, bf16[4,512,64]{2,1,0:T(8,1...) while((s32[]{:T(128)}, f32[2048,64]{0,1:T(8,128)S(1)}, ...), condition=%wide.region_22.22_spmd.clone, body=%wide.region_18.21_spmd.clone.sunk | while | flops 692584960 | bytes 73566400 | solution.py:91
  892.1 77.4 %all-reduce.1 = (f32[2,768]{1,0:T(2,128)S(1)}, f32[4,768]{1,0:T(4,128)S(1)}, f32[2,1536]{1,0:T(2,128)S(1)}) all-reduce(f32[2,768]{1,0:T(2,128)S(1)} %pad_maximum_fusion.4, f32[4,768]{1,0:T(4,128)S(1)} %pad_maximum_fusion.3, f32[2,1536]{1,0:T(2,128)S(1)} %broadcast_multiply_fusion), channel_id=1, replica_groups=mesh['dp'=16,'tensor'=2] {'dp'}, use_global_device_ids=true, to_apply=%region_31.32 | all-reduce | flops 7680 | bytes 61440 | tf_op jit(solution)/shard_map/psum | solution.py:216
  974.2 59.4 %all-reduce.5.cloned.1.call-done = f32[3,768,384]{2,0,1:T(4,128)} async-done(((f32[3,768,384]{2,0,1:T(4,128)}), f32[3,768,384]{2,0,1:T(4,128)}) %all-reduce.5.cloned.1.call-update) | async-done | bytes 3538960
  1049.7 141.5 %reduce-scatter.20.cloned.1.call-done = f32[1536,48]{0,1:T(8,128)} async-done(((f32[1536,768]{0,1:T(8,128)}), f32[1536,48]{0,1:T(8,128)}) %reduce-scatter.20.cloned.1.call-update) | async-done | bytes 294928 | tf_op jit(solution)/shard_map/reduce_scatter | solution.py:198
  1191.2 141.6 %reduce-scatter.18.cloned.1.call-done = f32[48,1536]{1,0:T(8,128)} async-done(((f32[768,1536]{1,0:T(8,128)}), f32[48,1536]{1,0:T(8,128)}) %reduce-scatter.18.cloned.1.call-update) | async-done | bytes 294928 | tf_op jit(solution)/shard_map/reduce_scatter | solution.py:197
  1332.8 128.7 %reduce-scatter.16.cloned.1.call-done = f32[384,48]{0,1:T(8,128)} async-done(((f32[384,768]{0,1:T(8,128)}), f32[384,48]{0,1:T(8,128)}) %reduce-scatter.16.cloned.1.call-update) | async-done | bytes 73744 | tf_op jit(solution)/shard_map/reduce_scatter | solution.py:196
  (659 shorter events, 690.6 us)
Async XLA Ops:
  7.2 50.8 %all-gather.10.cloned.1.call-start = ((), (), s32[]{:S(2)}) async-start(), calls=%async_computation.8 | async-start | bytes 4718592 | tf_op jit(solution)/shard_map/all_gather | solution.py:104
  7.9 79.5 %all-gather.8.cloned.1.call-start = ((), (), s32[]{:S(2)}) async-start(), calls=%async_computation.7 | async-start | bytes 1880064 | tf_op jit(solution)/shard_map/all_gather | solution.py:106
  8.7 222.9 %reduce-scatter.8.cloned.1.call-start = ((), (), s32[]{:S(2)}) async-start(), calls=%async_computation.9 | async-start | bytes 9437184 | tf_op jit(solution)/shard_map/reduce_scatter | solution.py:120
  218.1 80.0 %all-gather.14.cloned.1.call-start = ((), (), s32[]{:S(2)}) async-start(), calls=%async_computation.11 | async-start | bytes 2506752 | tf_op jit(solution)/shard_map/all_gather | solution.py:133
  218.7 92.4 %all-gather.12.cloned.1.call-start = ((), (), s32[]{:S(2)}) async-start(), calls=%async_computation.10 | async-start | bytes 4718592 | tf_op jit(solution)/shard_map/all_gather | solution.py:131
  237.2 140.4 %all-gather.16.cloned.1.call-start = ((), (), s32[]{:S(2)}) async-start(), calls=%async_computation.12 | async-start | bytes 2506752 | tf_op jit(solution)/shard_map/all_gather | solution.py:134
  237.8 163.0 %reduce-scatter.10.cloned.1.call-start = ((), (), s32[]{:S(2)}) async-start(), calls=%async_computation.13 | async-start | bytes 9437184 | tf_op jit(solution)/shard_map/reduce_scatter | solution.py:142
  387.3 39.3 %all-gather.18.cloned.1.call-start = ((), (), s32[]{:S(2)}) async-start(), calls=%async_computation.14 | async-start | bytes 4718592 | tf_op jit(solution)/shard_map/all_gather | solution.py:155
  413.2 56.4 %reduce-scatter.12.cloned.1.call-start = ((), (), s32[]{:S(2)}) async-start(), calls=%async_computation.15 | async-start | bytes 9437184 | tf_op jit(solution)/shard_map/reduce_scatter | solution.py:162
  426.6 20.2 %copy-start.24 = (bf16[768,1536]{1,0:T(8,128)(2,1)S(1)}, bf16[768,1536]{1,0:T(8,128)(2,1)}, u32[]{:S(2)}) copy-start(bf16[768,1536]{1,0:T(8,128)(2,1)} %all-gather.14.cloned.1.call-done) | copy-start | bytes 7077892
  453.8 20.1 %copy-start.11 = (f32[1024]{0:T(1024)S(1)}, f32[1024]{0:T(1024)}, u32[]{:S(2)}) copy-start(f32[1024]{0:T(1024)} %copy-done.10) | copy-start | bytes 12292
  453.8 38.8 %all-gather.20.cloned.1.call-start = ((), (), s32[]{:S(2)}) async-start(), calls=%async_computation.16 | async-start | bytes 4718592 | tf_op jit(solution)/shard_map/all_gather | solution.py:171
  477.0 15.6 %copy-start.7 = (bf16[384,768]{0,1:T(8,128)(2,1)S(1)}, bf16[384,768]{0,1:T(8,128)(2,1)}, u32[]{:S(2)}) copy-start(bf16[384,768]{0,1:T(8,128)(2,1)} %all_gather.26) | copy-start | bytes 1769476
  479.2 554.4 %all-reduce.5.cloned.1.call-start = ((), (), s32[]{:S(2)}) async-start(), calls=%async_computation.21 | async-start | bytes 9437184
  852.4 193.8 %reduce-scatter.14.cloned.1.call-start = ((), (), s32[]{:S(2)}) async-start(), calls=%async_computation.17 | async-start | bytes 4718592 | tf_op jit(solution)/shard_map/reduce_scatter | solution.py:202
  862.1 329.1 %reduce-scatter.20.cloned.1.call-start = ((), (), s32[]{:S(2)}) async-start(), calls=%async_computation.20 | async-start | bytes 5013504 | tf_op jit(solution)/shard_map/reduce_scatter | solution.py:198
  873.5 459.3 %reduce-scatter.18.cloned.1.call-start = ((), (), s32[]{:S(2)}) async-start(), calls=%async_computation.19 | async-start | bytes 5013504 | tf_op jit(solution)/shard_map/reduce_scatter | solution.py:197
  885.1 6.9 copy-start.18
  885.1 7.0 copy-start.17
  885.1 7.0 copy-start.13
  885.1 7.0 copy-start.12
  885.1 161.1 %copy-start.9 = (f32[1024]{0:T(1024)S(1)}, f32[1024]{0:T(1024)}, u32[]{:S(2)}) copy-start(f32[1024]{0:T(1024)} %copy-done.8) | copy-start | bytes 12292
  885.1 576.4 %reduce-scatter.16.cloned.1.call-start = ((), (), s32[]{:S(2)}) async-start(), calls=%async_computation.18 | async-start | bytes 1253376 | tf_op jit(solution)/shard_map/reduce_scatter | solution.py:196
  885.2 161.1 %copy-start.3 = (f32[1024,768]{1,0:T(8,128)S(1)}, f32[1024,768]{1,0:T(8,128)}, u32[]{:S(2)}) copy-start(f32[1024,768]{1,0:T(8,128)} %copy-done.2) | copy-start | bytes 9437188
  (67 other events, 198.9 us)
Sparse Core Ops, SparseCore 0:
  9.6 14.8 all-gather.9
  27.1 60.2 all-gather.7
  218.3 13.2 reduce-scatter.7
  234.6 63.4 all-gather.13
  300.1 10.9 all-gather.11
  314.1 63.4 all-gather.15
  387.4 13.3 reduce-scatter.9
  413.3 13.2 all-gather.17
  453.9 15.6 reduce-scatter.11
  479.3 13.2 all-gather.19
  852.5 181.0 all-reduce.4
  1036.2 9.9 reduce-scatter.13
  1052.8 138.3 reduce-scatter.19
  1196.8 135.9 reduce-scatter.17
  1338.7 122.7 reduce-scatter.15
